TPU v7x, 32 devices: a whole 2x2x4 slice. The times are simulated.
32 devices in a mesh: section: 2 (over core), batch: 4 (over y, x), rows: 4 (over z).
Axes of the slice: x: 2, y: 2, z: 4, core: 2. Of those that a mesh axis runs over, the one named last changes fastest.
Arguments:
- inputs: float32 [4, 4, 256, 64, 256], P(None, 'batch', 'rows'), may hold values from -6 to 6
- cotangent: float32 [4, 4, 256, 64, 256], P(None, 'batch', 'rows'), may hold values from -6 to 6
- region_id: int32 [4, 4, 256, 256], P(None, 'batch', 'rows'), may hold values from 0 to 8, as said below
- spectral_w: float32 [2, 64, 64, 64, 128], P('section', 'rows'), may hold values from -1 to 1
- conv_w: float32 [2, 64, 64], P('section'), may hold values from -0.75 to 0.75
- bias_vector: float32 [2, 64], P('section'), may hold values from -3 to 3
Outputs:
- boundary: float32 [2, 4, 4, 256, 64, 256], P('section', None, 'batch', 'rows')
- spectral_grad: float32 [2, 64, 64, 64, 128], P('section', 'rows')
- conv_grad: float32 [2, 64, 64], P('section')
- bias_grad: float32 [2, 64], P('section')
- layer_rms: float32 [2, 2, 8], P('section')
Inputs may be any that keep to these rules, and one draw needn't show every extreme that they name: `region_id`: 0 marks land, 1 to 8 the subregion of a sea pixel; the first column of every grid is sea and holds every subregion.
All inputs are finite; a program needn't handle non-finite values.
Results may differ from a plain program's by a relative error of at most 0.0003.
Values sent between devices are 32-bit elements; how exact they have to be, the bound alone decides.
A program may use at most 832 MiB of HBM per device.

v0:
```python
import functools
import math
import types

import jax
import jax.numpy as jnp
import numpy as np
from jax import lax
from jax.experimental import pallas as pl
from jax.experimental.pallas import tpu as pltpu
from jax.sharding import PartitionSpec as P

R = 8
G = 8
AHEAD = 2
F32 = jnp.float32
BF16 = jnp.bfloat16
VMEM_LIMIT = 62 * 1024 * 1024
MESH = pl.DeviceIdType.MESH


def split(value):
    high = value.astype(BF16)
    return high, (value - high.astype(F32)).astype(BF16)


def dot(left, right, dims=(((1,), (0,)), ((), ()))):
    return lax.dot_general(left, right, dims, preferred_element_type=F32)


def dot3(left, right):
    return dot(left[0], right[0]) + (dot(left[1], right[0]) + dot(left[0], right[1]))


def np_split(value):
    high = value.astype(np.float32).astype(BF16)
    return high, (value - high.astype(np.float64)).astype(np.float32).astype(BF16)


def col_tables(width, half):
    phase = 2.0 * math.pi / width * (np.outer(np.arange(width), np.arange(half)) % width)
    cosine, sine = np.cos(phase) / math.sqrt(width), np.sin(phase) / math.sqrt(width)
    plain = np.concatenate([cosine, -sine, -sine, -cosine], 1)
    doubled = plain * np.tile(np.where(np.arange(half) == 0, 1.0, 2.0), 4)[None, :]
    return plain, doubled


def row_tables(height, mode_rows, first_row, rows_dev):
    position = jnp.arange(mode_rows, dtype=jnp.int32)
    frequency = jnp.where(position < mode_rows // 2, position, height - mode_rows + position)
    row = first_row + jnp.arange(rows_dev, dtype=jnp.int32)
    phase = 2.0 * math.pi / height * (frequency[:, None] * row[None, :] % height).astype(F32)
    small = jnp.concatenate([jnp.cos(phase), jnp.sin(phase)], 1) / math.sqrt(height)
    rounded = lax.reduce_precision(small, 8, 7)
    high, low = rounded.astype(BF16), (small - rounded).astype(BF16)
    forward = jnp.concatenate([jnp.concatenate([high, high], 1), jnp.concatenate([low, jnp.zeros_like(low)], 1)], 0)
    inverse = jnp.concatenate([high.T, high.T, low.T], 1)
    return forward, inverse


def to_modes(value, table, kron, spread, p_ref):
    mode_rows, count, lanes = p_ref.shape
    rows = value.shape[0] // count
    high, low = split(value)
    spectra = dot(jnp.concatenate([high, low, high], 1), table)
    for i in range(2):
        spread[i] = spectra[:, i * lanes:(i + 1) * lanes]
    out = p_ref.reshape(mode_rows * count, lanes)
    for first in range(0, count, 2):
        sides = []
        for c in (first, first + 1):
            pick = pl.ds(c, rows, stride=count)
            sides.append(jnp.concatenate([spread[i, pick, :] for i in range(2)], 0))
        high, low = split(jnp.concatenate(sides, 1))
        both = dot(kron, jnp.concatenate([high, low], 0))
        result = both[:mode_rows] + both[mode_rows:]
        for i in range(2):
            out[pl.ds(first + i, mode_rows, stride=count), :] = result[:, i * lanes:(i + 1) * lanes]


def from_modes(y_ref, table, kron, spread):
    mode_rows, count, lanes = y_ref.shape
    rows, pieces = spread.shape[1] // count, spread.shape[0]
    modes = y_ref.reshape(mode_rows * count, lanes)
    sides = []
    for first in range(0, count, 2):
        pair = [modes[pl.ds(c, mode_rows, stride=count), :] for c in (first, first + 1)]
        high, low = split(jnp.concatenate(pair, 1))
        both = dot(kron, jnp.concatenate([high, low, high], 0))
        for i in range(2):
            side = both[:, i * lanes:(i + 1) * lanes]
            sides.append(jnp.concatenate([side[:rows], side[rows:]], 1))
    high, low = split(jnp.concatenate(sides, 0))
    out = dot(jnp.concatenate([high, low, high], 1), table)
    for c in range(count):
        for i in range(pieces):
            spread[i, pl.ds(c, rows, stride=count), :] = out[c * rows:(c + 1) * rows, i * 128:(i + 1) * 128]
    return jnp.concatenate([spread[i] for i in range(pieces)], 1)


def gelu_parts(z):
    gauss = jnp.exp2((-0.5 / math.log(2.0)) * (z * z))
    base = 1.0 + (0.3275911 / math.sqrt(2.0)) * jnp.abs(z)
    t = pl.reciprocal(base, approx=True)
    t = t * (2.0 - base * t)
    poly = t * (0.127414796 + t * (-0.142248368 + t * (0.7107068705 + t * (-0.7265760135 + t * 0.5307027145))))
    tail = poly * gauss
    phi = jnp.where(z >= 0, 1.0 - tail, tail)
    return z * phi, phi + z * (gauss * (1.0 / math.sqrt(2.0 * math.pi)))


def flat(ref):
    rows, count, width = ref.shape
    return ref[...].reshape(rows * count, width)


def put(ref, value):
    ref[...] = value.reshape(ref.shape)


def place_and_peers():
    section, z = lax.axis_index("section"), lax.axis_index("rows")
    return section, z, lax.axis_size("rows")


def greet(section, z, n, lines, members=0):
    barrier = pltpu.get_barrier_semaphore()
    pl.semaphore_signal(barrier, inc=1, device_id={"section": 1 - section}, device_id_type=MESH)
    if not lines:
        pl.semaphore_wait(barrier, 1)
        return

    @pl.when(z > 0)
    def _():
        pl.semaphore_signal(barrier, inc=1, device_id={"rows": z - 1}, device_id_type=MESH)

    @pl.when(z < n - 1)
    def _():
        pl.semaphore_signal(barrier, inc=1, device_id={"rows": z + 1}, device_id_type=MESH)

    for away in range(1, members):
        pl.semaphore_signal(barrier, inc=1, device_id={"batch": lax.rem(lax.axis_index("batch") + away, members)},
                            device_id_type=MESH)

    others = 1 + max(members - 1, 0)
    pl.semaphore_wait(barrier, others + (z > 0).astype(jnp.int32) + (z < n - 1).astype(jnp.int32))


def to_core(src, dst, sems, section):
    return pltpu.make_async_remote_copy(src_ref=src, dst_ref=dst, send_sem=sems[0], recv_sem=sems[1],
                                        device_id={"section": 1 - section}, device_id_type=MESH)


def guard(condition, body):
    if isinstance(condition, (bool, np.bool_)):
        if condition:
            body()
    else:
        pl.when(condition)(body)


class Line:
    def __init__(self, section, z, n, chunks, send, recv):
        self.section, self.z, self.n, self.chunks = section, z, n, chunks
        self.send, self.recv = send, recv

    def move(self, way, q, hop, src, dst):
        return pltpu.make_async_remote_copy(
            src_ref=src, dst_ref=dst, send_sem=self.send.at[way, q, hop], recv_sem=self.recv.at[way, q, hop],
            device_id={"rows": self.z + 1 if way == 0 else self.z - 1}, device_id_type=MESH)

    def sends(self, way):
        return self.z < self.n - 1 if way == 0 else self.z > 0

    def hears(self, way):
        return self.z > 0 if way == 0 else self.z < self.n - 1


def within(value, count):
    return jnp.logical_and(value >= 0, value < count)


class Gather(Line):
    def __init__(self, section, z, n, r, parity):
        super().__init__(section, z, n, r.full.shape[1], r.send.at[parity], r.recv.at[parity])
        self.full, self.give_from = r.full.at[parity], r.y_give.at[parity]
        self.cross = r.y_cross.at[parity]

    def swap(self, q):
        return to_core(self.give_from.at[q], self.full.at[q, self.z, self.section],
                       (self.cross.at[0, q], self.cross.at[1, q]), self.section)

    def give(self, q):
        self.swap(q).start()

    def hop(self, way, q, hop):
        piece = self.full.at[q, self.source(way, hop)]
        return self.move(way, q, hop, piece, piece)

    def source(self, way, hop):
        return self.z - hop if way == 0 else self.z + hop

    def known(self, way, hop):
        at = self.source(way, hop)
        return at >= 0 if way == 0 else at < self.n

    def own(self, q):
        self.swap(q).wait_recv()
        for way in range(2):
            @pl.when(self.sends(way))
            def _():
                self.hop(way, q, 0).start()

    def step(self, q, hop):
        for way in range(2):
            @pl.when(self.known(way, hop + 1))
            def _():
                piece = self.full.at[q, self.source(way, hop + 1)]
                self.move(way, q, hop, piece, piece).wait_recv()

                @pl.when(self.sends(way))
                def _():
                    self.hop(way, q, hop + 1).start()

    def begin(self):
        for q in range(min(AHEAD, self.chunks)):
            self.own(q)

    def tick(self, t):
        @pl.when(t + AHEAD < self.chunks)
        def _():
            self.own(t + AHEAD)

        for hop in range(self.n - 1):
            q = t - hop - 1
            pl.when(within(q, self.chunks))(functools.partial(self.step, q, hop))

    def finish(self):
        def body(q, carry):
            self.swap(q).wait_send()
            for way in range(2):
                for hop in range(self.n - 1):
                    @pl.when(jnp.logical_and(self.sends(way), self.known(way, hop)))
                    def _():
                        self.hop(way, q, hop).wait_send()
            return carry

        lax.fori_loop(0, self.chunks, body, 0)


class Sum(Line):
    def __init__(self, section, z, n, r, parity, admit):
        super().__init__(section, z, n, r.part.shape[2], r.red_send.at[parity], r.red_recv.at[parity])
        self.part, self.come, self.keep, self.admit = r.part.at[parity], r.come.at[parity], r.keep.at[parity], admit

    def owner(self, way, hop):
        return self.z + self.n - hop if way == 0 else self.z - self.n + hop

    def valid(self, way, hop):
        return self.z <= hop - 1 if way == 0 else self.z >= self.n - hop

    def sent(self, way, q, hop):
        return self.move(way, q, hop, self.part.at[self.owner(way, hop), q], self.come.at[way, q, hop - 1])

    def heard(self, way, q, hop):
        come = self.come.at[way, q, hop - 1]
        self.move(way, q, hop, come, come).wait_recv()

    def first(self, q):
        self.admit(q)
        for way in range(2):
            @pl.when(jnp.logical_not(self.hears(way)))
            def _():
                for hop in range(1, self.n):
                    @pl.when(self.valid(way, hop))
                    def _():
                        self.sent(way, q, hop).start()

    def step(self, q, hop):
        for way in range(2):
            @pl.when(jnp.logical_and(self.valid(way, hop), self.hears(way)))
            def _():
                self.heard(way, q, hop - 1)
                owner = self.owner(way, hop)
                self.part[owner, q] = self.part[owner, q] + self.come[way, q, hop - 2]
                self.sent(way, q, hop).start()

    def final(self, q):
        for way in range(2):
            @pl.when(self.hears(way))
            def _():
                self.heard(way, q, self.n - 1)
                self.part[self.z, q] = self.part[self.z, q] + self.come[way, q, self.n - 2]

        self.keep[q] = self.part[self.z, q]

    def tick(self, t):
        pl.when(within(t, self.chunks))(functools.partial(self.first, t))
        for hop in range(2, self.n + 1):
            q = t - hop + 1
            pl.when(within(q, self.chunks))(
                functools.partial(self.step, q, hop) if hop < self.n else functools.partial(self.final, q))

    def finish(self):
        def body(q, carry):
            for way in range(2):
                for hop in range(1, self.n):
                    @pl.when(self.valid(way, hop))
                    def _():
                        self.sent(way, q, hop).wait_send()
            return carry

        lax.fori_loop(0, self.chunks, body, 0)


def fetch(src, dst, sem, parts=1):
    step = dst.shape[0] // parts
    for i in range(parts):
        pltpu.make_async_copy(src.at[pl.ds(i * step, step)], dst.at[pl.ds(i * step, step)], sem).start()


def arrived(dst, sem):
    pltpu.make_async_copy(dst, dst, sem).wait()


def portions(total, count):
    return [(i * total // count, (i + 1) * total // count) for i in range(count)]


def conv_rows(weight, bias, a, out, first, last):
    channels, width = a.shape[1:]
    block = weight.shape[0] // channels

    def body(i, carry):
        at = pl.ds(i * block, block)
        high, low = split(a[at].reshape(block * channels, width))
        result = dot(weight[...], jnp.concatenate([high, high, low], 0)).reshape(block, channels, width)
        out[at] = result + bias[...][None] if bias is not None else out[at] + result
        return carry

    lax.fori_loop(first, last, body, 0)


def grad_rows(a, gz, cg_ref, bg_ref, first, last):
    channels, width = a.shape[1:]

    def body(r, carry):
        grad, bias = carry
        g = gz[r]
        left = jnp.concatenate(split(a[r]), 0)
        right = jnp.concatenate(split(g), 0)
        return grad + dot(left, right, (((1,), (1,)), ((), ()))), bias + g

    grad, bias = lax.fori_loop(first, last, body, (cg_ref[...], bg_ref[...]))
    cg_ref[...] = grad
    bg_ref[...] = bias


def chunk_of(ref, q, count):
    rows, _, width = ref.shape
    return ref[:, pl.ds(pl.multiple_of(q * count, count), count), :].reshape(rows * count, width)


def chunk_at(ref, q, count):
    return ref.at[:, pl.ds(pl.multiple_of(q * count, count), count), :]


class Modes:
    def __init__(self, section, buffer, p_out, cross):
        self.section, self.buffer, self.p_out, self.cross = section, buffer, p_out, cross

    def view(self, q):
        n, halves, kx, count, lanes = self.buffer.shape[1:]
        return self.buffer.at[q].reshape(n * halves * kx, count, lanes)

    def cross_copy(self, q):
        return to_core(self.buffer.at[q, :, 1 - self.section], self.p_out.at[:, q, 1],
                       (self.cross.at[0, q], self.cross.at[1, q]), self.section)

    def start(self, q):
        self.cross_copy(q).start()
        self.p_out[:, q, 0] = self.buffer[q, :, self.section]

    def wait(self, q):
        self.cross_copy(q).wait()


class Bound:
    def __init__(self, section, owner, micro, other, source, bound, local, cross):
        self.section, self.owner, self.micro, self.other = section, owner, micro, other
        self.source, self.bound, self.local, self.cross = source, bound, local, cross

    def copies(self, q, count, micro):
        src, dst = chunk_at(self.source, q, count), chunk_at(self.bound.at[micro], q, count)
        return (pltpu.make_async_copy(src, dst, self.local.at[q]),
                to_core(src, dst, (self.cross.at[0, q], self.cross.at[1, q]), self.section))

    def start(self, q, count):
        here, there = self.copies(q, count, self.micro)

        @pl.when(self.section == self.owner)
        def _():
            here.start()

        @pl.when(self.section != self.owner)
        def _():
            there.start()

    def wait(self, q, count):
        here, there = self.copies(q, count, self.micro)
        come = self.copies(q, count, self.other)[1]

        @pl.when(self.section == self.owner)
        def _():
            here.wait()
            come.wait_recv()

        @pl.when(self.section != self.owner)
        def _():
            there.wait_send()


def add_squares(value, total):
    rows, _, width = total.shape
    square = (value * value).reshape(rows, -1, width)
    for at in range(0, square.shape[1], G):
        total[...] += square[:, at:at + G]


def region_sums(rid_ref, eo, eb, stat_ref):
    rows, _, width = eo.shape
    rid = rid_ref[...]
    energies = (jnp.sum(eo[...], axis=1), jnp.sum(eb[...], axis=1), jnp.ones((rows, width), F32))
    for kind in range(3):
        for region in range(R):
            line = jnp.sum(jnp.where(rid == region + 1, energies[kind], 0.0), axis=0, keepdims=True)
            total = line[:, :128]
            for piece in range(1, width // 128):
                total = total + line[:, piece * 128:(piece + 1) * 128]
            stat_ref[kind, region:region + 1, :] = total


class Share:
    def __init__(self, r, index, parity):
        self.r, self.index, self.parity = r, index, parity
        self.me, self.members = lax.axis_index("batch"), lax.axis_size("batch")

    def copies(self):
        source, target = self.r.keep.at[self.parity], getattr(self.r, f"shared{self.index}").at[self.me]
        yield pltpu.make_async_copy(source, target, self.r.s_local.at[self.parity])
        for away in range(1, self.members):
            yield pltpu.make_async_remote_copy(
                src_ref=source, dst_ref=target, send_sem=self.r.s_send.at[self.parity, away],
                recv_sem=self.r.s_recv.at[self.index, away],
                device_id={"batch": lax.rem(self.me + away, self.members)}, device_id_type=MESH)

    def start(self):
        for copy in self.copies():
            copy.start()

    def wait_send(self):
        for i, copy in enumerate(self.copies()):
            if i == 0:
                copy.wait()
            else:
                copy.wait_send()

    def wait_recv(self):
        for i, copy in enumerate(self.copies()):
            if i > 0:
                copy.wait_recv()


class Head:
    def __init__(self, micro, place, parity, section, r):
        self.r, self.field, self.sem = r, r.fields.at[place], r.field_sem.at[place]
        self.source, self.count = r.inputs.at[micro, 0], r.full.shape[5]
        self.modes = Modes(section, r.p_buf, r.part.at[parity], r.p_cross.at[parity])

    def fetch(self):
        fetch(self.source, self.field, self.sem, 4)

    def got(self):
        arrived(self.field, self.sem)

    def chunk(self, q):
        r = self.r
        to_modes(chunk_of(self.field, q, self.count), r.t_plain[...], r.kron[...], r.spread, self.modes.view(q))
        self.modes.start(q)


class Stage:
    def __init__(self, k, kind, j, per_core, places, section, z, n, r):
        self.k, self.kind, self.j, self.r, self.section, self.n = k, kind, j, r, section, n
        self.parity = k % 2
        self.micro, self.other = section * per_core + j, (1 - section) * per_core + j
        self.forward, self.last = kind in ("middle", "turn"), kind == "tail"
        self.buffers = {name: r.fields.at[i] for name, i in places.items()}
        self.sems = {name: r.field_sem.at[i] for name, i in places.items()}
        self.gather = Gather(section, z, n, r, self.parity)
        self.count, self.lanes = r.full.shape[5], r.full.shape[6]
        self.chunks = r.full.shape[1]
        plain = lambda name: getattr(r, f"{name}{j}")
        if kind == "middle":
            self.loads = dict(a=r.inputs.at[self.micro, 0])
            self.saves = dict(a=plain("a1_"), z=plain("dg0_"))
        elif kind == "turn":
            self.loads = dict(a=plain("a1_"), cot=r.cotangent.at[self.micro, 0])
            self.saves = dict(cot=plain("gz1_"))
        elif kind == "back":
            self.loads = dict(gz=plain("gz1_"), h=r.cotangent.at[self.micro, 0], a=plain("a1_"), dg=plain("dg0_"))
            self.saves = dict(h=plain("ga1_"), dg=plain("gz0_"))
        else:
            self.loads = dict(gz=plain("gz0_"), h=plain("ga1_"), a=r.inputs.at[self.micro, 0])
            self.saves = {}
        layer = 0 if kind in ("middle", "tail") else 1
        self.weight, self.bias = r.conv.at[layer if self.forward else 2 + layer], r.bias.at[layer]
        self.table = r.t_plain if kind == "middle" else r.t_doubled
        self.itable = r.it_doubled if self.forward else r.it_plain
        if not self.last:
            self.modes = Modes(section, r.p_buf, r.part.at[self.parity], r.p_cross.at[self.parity])
        if kind in ("turn", "tail"):
            self.bound = Bound(section, 1 if kind == "turn" else 0, self.micro, self.other,
                               self.buffers["a" if kind == "turn" else "h"], r.bound,
                               r.b_local.at[self.parity], r.b_cross.at[self.parity])

    def prefetch(self):
        for name, src in self.loads.items():
            if self.kind != "middle":
                fetch(src, self.buffers[name], self.sems[name])
        if self.forward:
            self.rid_copy().start()

    def rid_copy(self):
        return pltpu.make_async_copy(self.r.region.at[self.micro, 0], self.r.rid.at[self.parity],
                                     self.r.rid_sem.at[self.parity])

    def got(self, name):
        arrived(self.buffers[name], self.sems[name])

    def open(self):
        r, b = self.r, self.buffers
        if self.forward:
            r.eo[...] = jnp.zeros_like(r.eo)
            r.eb[...] = jnp.zeros_like(r.eb)
            if self.kind != "middle":
                self.got("a")
        else:
            for name in ("gz", "h", "a"):
                self.got(name)
            at = self.k - self.r.first_back
            r.cg[at] = jnp.zeros_like(r.cg[at])
            r.bg[at] = jnp.zeros_like(r.bg[at])

    def before(self, i):
        r, b = self.r, self.buffers
        a = b["a"]
        rows, channels = a.shape[:2]
        blocks, parts = rows // (self.weight.shape[0] // channels), self.n - 1
        span = (i * blocks // parts, (i + 1) * blocks // parts)
        if self.forward:
            conv_rows(self.weight, self.bias, a, b["z"], *span)
        else:
            conv_rows(self.weight, None, b["gz"], b["h"], *span)
            at = self.k - r.first_back
            grad_rows(a, b["gz"], r.cg.at[at], r.bg.at[at], i * rows // parts, (i + 1) * rows // parts)

    def outs(self, q):
        return [pltpu.make_async_copy(chunk_at(self.buffers[name], q, self.count), chunk_at(dst, q, self.count),
                                      self.r.out_sem.at[self.parity, i, q])
                for i, (name, dst) in enumerate(self.saves.items())]

    def late(self):
        for name in ("cot", "dg"):
            if name in self.loads:
                self.got(name)

    def chunk(self, q):
        r, b, count = self.r, self.buffers, self.count
        spectral = from_modes(self.gather.full.at[q].reshape(-1, count, self.lanes), self.itable[...], r.ikron[...],
                              r.spread)
        if self.forward:
            branch, slope = gelu_parts(spectral + chunk_of(b["z"], q, count))
            if self.kind == "turn":
                put(chunk_at(b["cot"], q, count), chunk_of(b["cot"], q, count) * slope)
            else:
                put(chunk_at(b["z"], q, count), slope)
            add_squares(branch, r.eb)
            out = chunk_of(b["a"], q, count) + branch
            put(chunk_at(b["a"], q, count), out)
            add_squares(out, r.eo)
            source = b["cot" if self.kind == "turn" else "a"]
        else:
            ga = spectral + chunk_of(b["h"], q, count)
            put(chunk_at(b["h"], q, count), ga)
            if not self.last:
                put(chunk_at(b["dg"], q, count), ga * chunk_of(b["dg"], q, count))
                source = b["dg"]
        for copy in self.outs(q):
            copy.start()
        if self.kind in ("turn", "tail"):
            self.bound.start(q, count)
        if not self.last:
            to_modes(chunk_of(source, q, count), self.table[...], r.kron[...], r.spread, self.modes.view(q))

            pl.when(q == self.chunks - 1)(self.gather.finish)
            self.modes.start(q)

    def end(self):
        if self.forward:
            self.rid_copy().wait()
            region_sums(self.r.rid.at[self.parity], self.r.eo, self.r.eb, self.r.stat.at[self.k])
        if self.last:
            self.gather.finish()

    def close(self):
        def body(q, carry):
            for copy in self.outs(q):
                copy.wait()
            if self.kind in ("turn", "tail"):
                self.bound.wait(q, self.count)
            return carry

        lax.fori_loop(0, self.chunks, body, 0)


def stages_kernel(per_core, kinds, places, mixes, r):
    section, z, n = place_and_peers()
    chunks, count = r.full.shape[1], r.full.shape[5]
    r.first_back = 2 * per_core
    stages = [Stage(k, kind, j, per_core, places[k], section, z, n, r)
              for k, (kind, j) in enumerate((kind, j) for kind in kinds for j in range(per_core))]
    heads = [Head(section * per_core + j, places[j]["a"], j, section, r) for j in range(per_core)]
    half = r.far.shape[0]

    def spare(q, x):
        groups = r.fields.shape[1] // count
        at = q * half + x
        place, at = 3 + at // (2 * groups), at % (2 * groups)
        side, group = at // groups, at % groups
        return r.fields.at[place, pl.ds(pl.multiple_of(group * count, count), count), :,
                           pl.ds(pl.multiple_of(side * 128, 128), 128)]

    def lend_in(q, x):
        rows = pl.ds(q * count, count)
        return pltpu.make_async_copy(r.weights.at[0, (1 - section) * half + x, rows], spare(q, x), r.w_load.at[q, x])

    def lent(q, x):
        return to_core(spare(q, x), r.far.at[x, pl.ds(q * count, count)],
                       (r.w_cross.at[0, q, x], r.w_cross.at[1, q, x]), section)

    blocks = [(q, x) for q in range(chunks) for x in range(half)]
    for head in heads:
        head.fetch()
    for block in blocks:
        lend_in(*block).start()
    greet(section, z, n, True, lax.axis_size("batch"))
    wide = r.full.at[1].reshape(-1, *r.wide_own.shape)
    small = [to_core(wide.at[section], wide.at[section], (r.m_cross.at[0, 0], r.m_cross.at[1, 0]), section),
             to_core(r.bias.at[section], r.bias.at[section], (r.m_cross.at[0, 1], r.m_cross.at[1, 1]), section)]
    wide[section] = r.wide_own[...]
    r.bias[section] = r.bias_own[...]
    for copy in small:
        copy.start()
    ahead, sums = [Sum(section, z, n, r, j, heads[j].modes.wait) for j in range(2)]
    mix = Mix(section, z, *mixes[0], ahead, stages[0].gather, r, lent)
    heads[0].got()

    def opening(q, carry):
        ahead.tick(q - 1)
        heads[0].chunk(q)

        @pl.when(q == 0)
        def _():
            for block in blocks:
                lend_in(*block).wait()
                lent(*block).start()

        return carry

    lax.fori_loop(0, chunks, opening, 0)
    for copy in small:
        copy.wait()
    for way in range(2):
        for layer in range(2):
            high, low = split(jnp.concatenate([wide[layer, way, side] for side in range(wide.shape[2])], 1))
            r.conv[2 * way + layer] = jnp.concatenate([high, low, high], 1)
    heads[1].got()
    mix.prime()

    def second(q, carry):
        ahead.tick(q + chunks - 1)

        @pl.when(q < chunks)
        def _():
            heads[1].chunk(q)

        sums.tick(q - 1)
        pl.when(within(q + chunks - n, chunks))(lambda: mix.chunk(q + chunks - n))
        return carry

    lax.fori_loop(0, n, second, 0)
    ahead.finish()
    mix.finish()
    shares = [Share(r, 0, 0)]
    shares[0].start()
    for block in blocks:
        lent(*block).wait_send()
    stages[0].prefetch()
    for k, stage in enumerate(stages):
        gather = stage.gather
        now = None if stage.last else Sum(section, z, n, r, stage.parity, stage.modes.wait)
        mix = None
        if sums is not None:
            mix = Mix(section, z, *mixes[(k + 1) // per_core], sums, stages[k + 1].gather, r)
            share = Share(r, k + 1, 1 - stage.parity)
            if k >= 1:
                shares[k - 1].wait_send()
            shares.append(share)
            mix.prime()
        lead = n - 1 if k == 0 else chunks - 1
        ready = n - 1 - lead
        gather.begin()
        stage.open()

        def early(i, carry):
            if sums is not None:
                sums.tick(i + lead)
            gather.tick(i)
            stage.before(i)
            if mix is not None and not mix.flip:
                pl.when(within(i - ready, chunks))(lambda: mix.chunk(i - ready))
            return carry

        lax.fori_loop(0, n - 1, early, 0)
        if k > 0:
            stages[k - 1].close()
        if k + 1 < len(stages):
            stages[k + 1].prefetch()
        stage.late()

        def later(q, carry):
            i = q + n - 1
            if sums is not None:
                sums.tick(i + lead)
            if now is not None:
                now.tick(i - n)
            gather.tick(i)
            stage.chunk(q)
            if mix is not None:
                if mix.flip:
                    pl.when(q == 0)(sums.finish)
                    mix.chunk(q)
                else:
                    pl.when(within(i - ready, chunks))(lambda: mix.chunk(i - ready))
            return carry

        lax.fori_loop(0, chunks, later, 0)
        if mix is not None:
            if not mix.flip:
                sums.finish()
            mix.finish()
            share.start()
        stage.end()
        sums = now
    stages[-1].close()
    for share in shares[-2:]:
        share.wait_send()
    for share in shares:
        share.wait_recv()


def swap_halves(value):
    return pltpu.roll(value, value.shape[-1] // 2, value.ndim - 1)


def left_lanes(shape):
    return lax.broadcasted_iota(jnp.int32, shape, len(shape) - 1) < shape[-1] // 2


def pieces(array):
    return [array[at:at + G] for at in range(0, array.shape[0], G)]


def spread_row(ref, row):
    return ref[pl.ds(row, G, stride=0), :]


class Mix:
    def __init__(self, section, z, layer, flip, sums, gather, r, lent=None):
        self.lent = lent
        self.section, self.z, self.layer, self.flip, self.r = section, z, layer, flip, r
        self.sums, self.gather = sums, gather
        self.chunks, self.grids, self.half, self.count, self.lanes = sums.part.shape[1:]
        self.channels, self.slots = r.weights.shape[2], r.wbuf.shape[0]
        self.blocks = self.chunks * self.half // 2

    def begin(self, block):
        per = self.half // 2
        q, x = block // per, 2 * (block % per)
        slot = lax.rem(block, self.slots)
        rows = pl.ds(q * self.count, self.count)
        if self.lent is not None:
            for at in range(2):
                self.lent(q, x + at).wait_recv()

        @pl.when(self.section == self.layer)
        def _():
            pltpu.make_async_copy(self.r.weights.at[0, pl.ds(self.section * self.half + x, 2), rows],
                                  self.r.wbuf.at[slot], self.r.wsem.at[slot]).start()

        @pl.when(self.section != self.layer)
        def _():
            pltpu.make_async_copy(self.r.far.at[pl.ds(x, 2), rows], self.r.wbuf.at[slot], self.r.wsem.at[slot]).start()

    def prime(self):
        for block in range(min(self.slots, self.blocks)):
            self.begin(jnp.int32(block))
        if not self.flip:
            self.r.macc[...] = jnp.zeros_like(self.r.macc)

    def chunk(self, q):
        def body(x, carry):
            block = q * (self.half // 2) + x // 2
            slot = lax.rem(block, self.slots)

            @pl.when(lax.rem(x, 2) == 0)
            def _():
                arrived(self.r.wbuf.at[slot], self.r.wsem.at[slot])

            (self.transposed if self.flip else self.forward)(q, x, self.r.wbuf.at[slot, lax.rem(x, 2)])

            @pl.when(jnp.logical_and(lax.rem(x, 2) == 1, block + self.slots < self.blocks))
            def _():
                self.begin(block + self.slots)

            return carry

        lax.fori_loop(0, self.half, body, 0)
        if self.flip:
            self.gather.give(q)

    def forward(self, q, x, weight):
        sides, groups = 2 * self.grids, self.channels // G
        total, source = self.r.macc.at[x], self.r.msrc
        for g in range(self.grids):
            value = self.sums.part[self.z, q, g, x]
            source[2 * g, :self.count] = value
            source[2 * g + 1, :self.count] = swap_halves(value)
        keys = [(k, o) for k in range(sides) for o in range(groups)]

        def body(octet, acc):
            acc = dict(zip(keys, acc))
            for u in range(G):
                i = octet * G + u
                rows = [spread_row(source.at[k], i) for k in range(sides)]
                for o in range(groups):
                    w = weight[i, o * G:(o + 1) * G, :]
                    for k in range(sides):
                        acc[k, o] = acc[k, o] + rows[k] * w
            return tuple(acc[key] for key in keys)

        acc = lax.fori_loop(0, self.count // G, body, tuple(total[k, o * G:(o + 1) * G, :] for k, o in keys))
        for key, value in zip(keys, acc):
            total[key[0], key[1] * G:(key[1] + 1) * G, :] = value

    def transposed(self, q, x, weight):
        sides, groups = 2 * self.grids, self.channels // G
        source = self.r.msrc
        for g in range(self.grids):
            value = jnp.concatenate([self.sums.part[self.z, at, g, x] for at in range(self.chunks)], 0)
            source[2 * g] = value
            source[2 * g + 1] = swap_halves(value)
        rows = [pieces(source[k]) for k in range(sides)]
        out = [[] for _ in range(sides)]
        for i in range(self.count):
            total = [None] * sides
            for o in range(groups):
                w = weight[i, o * G:(o + 1) * G, :]
                for k in range(sides):
                    term = w * rows[k][o]
                    total[k] = term if total[k] is None else total[k] + term
            for k in range(sides):
                out[k].append(jnp.sum(total[k], axis=0, keepdims=True))
        left = left_lanes((self.count, self.lanes))
        for g in range(self.grids):
            a, b = [jnp.concatenate(out[2 * g + side], 0) for side in range(2)]
            self.put(g, q, x, jnp.where(left, a + swap_halves(a), swap_halves(b) - b))

    def put(self, g, q, x, value):
        if g == 0:
            self.gather.full[q, self.z, self.section, x] = value
        else:
            self.gather.give_from[q, x] = value

    def finish(self):
        if self.flip:
            return
        left = left_lanes((self.channels, self.lanes))

        def body(x, carry):
            for g in range(self.grids):
                a, b = [self.r.macc[x, 2 * g + side] for side in range(2)]
                result = jnp.where(left, a - swap_halves(a), b + swap_halves(b))
                for q in range(self.chunks):
                    self.put(g, q, x, result[q * self.count:(q + 1) * self.count])
            return carry

        lax.fori_loop(0, self.half, body, 0)
        for q in range(self.chunks):
            self.gather.give(q)


def gather_columns(f_ref, d_ref, left_of, right_of):
    channels = f_ref.shape[2] * f_ref.shape[5]
    lanes = f_ref.shape[6]
    left = left_lanes((channels, lanes))
    for stream in range(f_ref.shape[0]):
        for member in range(f_ref.shape[1]):
            for g in range(f_ref.shape[3]):
                at = (stream * f_ref.shape[1] + member) * f_ref.shape[3] + g
                both = []
                for x in range(2):
                    f = f_ref[stream, member, :, g, x].reshape(channels, lanes)
                    turned = swap_halves(f)
                    left_of[x, at] = jnp.concatenate([f, jnp.where(left, -turned, turned)], 0).T
                    both.append(d_ref[stream, member, :, g, x].reshape(channels, lanes))
                right_of[at] = jnp.concatenate(both, 0).T


def column_products(left_of, right_of, product):
    grids, double, lanes = right_of.shape
    half = double // 2
    left = left_lanes((2 * grids, lanes))
    rows = right_of.reshape(grids * double, lanes)
    sides = [left_of.at[x].reshape(grids * double, lanes) for x in range(2)]

    def body(k, carry):
        pick = pl.ds(k, 2 * grids, stride=half)
        d = rows[pick, :]
        f_high, f_low = split(jnp.concatenate([side[pick, :] for side in sides], 0))
        d_high, d_low = split(jnp.concatenate([jnp.where(left, d, 0.0), jnp.where(left, 0.0, d)], 0))
        product[k] = dot(jnp.concatenate([f_high, f_low, f_high], 0), jnp.concatenate([d_high, d_high, d_low], 0),
                         (((0,), (0,)), ((), ())))
        return carry

    lax.fori_loop(0, half, body, 0, unroll=4)


def product_rows(product, first, out):
    half, double, lanes = product.shape
    channels = double // 2
    rows = product.reshape(half * double, lanes)

    def body(i, carry):
        parts = [rows[pl.ds(part * channels + first + i, half, stride=double), :] for part in range(2)]
        tile = jnp.concatenate(parts, 0).T
        for x in range(2):
            out[x, i] = tile[x * channels:(x + 1) * channels]
        return carry

    lax.fori_loop(0, out.shape[1], body, 0, unroll=4)


class GradInput:
    def __init__(self, first, f, g, fbuf, gbuf, sem):
        self.first, self.f, self.g, self.fbuf, self.gbuf, self.sem = first, f, g, fbuf, gbuf, sem

    def load(self, x, slot):
        for layer, condition in enumerate((self.first, jnp.logical_not(self.first))):
            @pl.when(condition)
            def _():
                for j in range(len(self.f[layer])):
                    pltpu.make_async_copy(self.f[layer][j].at[:, :, :, pl.ds(2 * x, 2)], self.fbuf.at[slot, j],
                                          self.sem.at[0, slot]).start()
                    pltpu.make_async_copy(self.g[layer][j].at[:, :, :, pl.ds(2 * x, 2)], self.gbuf.at[slot, j],
                                          self.sem.at[1, slot]).start()

    def next(self, x, count):
        slot = lax.rem(x, 2)

        @pl.when(x + 1 < count)
        def _():
            self.load(x + 1, 1 - slot)

        arrived(self.fbuf.at[slot], self.sem.at[0, slot])
        arrived(self.gbuf.at[slot], self.sem.at[1, slot])
        return self.fbuf.at[slot], self.gbuf.at[slot]


def grad_input(r, first, per_core):
    f = [[getattr(r, f"f{layer}{j}") for j in range(per_core)] for layer in range(2)]
    g = [[getattr(r, f"g{layer}{j}") for j in range(per_core)] for layer in range(2)]
    return GradInput(first, f, g, r.fbuf, r.gbuf, r.in_sem)


def far_grad_kernel(per_core, r):
    section, z, n = place_and_peers()
    pairs, block = r.far.shape[0] // 2, r.out.shape[2]
    blocks = r.far.shape[1] // block
    source = grad_input(r, section != 0, per_core)

    def move(k, slot):
        p, i = k // blocks, k % blocks
        return to_core(r.out.at[slot], r.far.at[pl.ds(2 * p, 2), pl.ds(i * block, block)], (r.send.at[k], r.recv.at[k]),
                       section)

    source.load(0, 0)
    greet(section, z, n, False)

    def body(p, carry):
        gather_columns(*source.next(p, pairs), r.left_of, r.right_of)
        column_products(r.left_of, r.right_of, r.product)

        def inner(i, carry):
            k = p * blocks + i

            @pl.when(k >= 2)
            def _():
                move(k - 2, lax.rem(k, 2)).wait_send()

            product_rows(r.product, i * block, r.out.at[lax.rem(k, 2)])
            move(k, lax.rem(k, 2)).start()
            return carry

        return lax.fori_loop(0, blocks, inner, carry)

    lax.fori_loop(0, pairs, body, 0)
    total = pairs * blocks
    for k in (total - 2, total - 1):
        move(k, k % 2).wait_send()

    def close(k, carry):
        move(k, 0).wait_recv()
        return carry

    lax.fori_loop(0, total, close, 0)


def own_grad_kernel(names, per_core, m_ref, *refs):
    r = types.SimpleNamespace(**dict(zip(names, refs)))
    p, i = pl.program_id(0), pl.program_id(1)
    source = grad_input(r, m_ref[0] == 0, per_core)

    @pl.when(i == 0)
    def _():
        @pl.when(p == 0)
        def _():
            source.load(0, 0)

        gather_columns(*source.next(p, pl.num_programs(0)), r.left_of, r.right_of)
        column_products(r.left_of, r.right_of, r.product)

    r.bound_out[...] = r.bound_in[...]
    r.out[1 - m_ref[0]] = r.far[...]
    product_rows(r.product, i * r.out.shape[2], r.out.at[m_ref[0]])


def whole(array):
    return pl.BlockSpec(array.shape, lambda *_: (0,) * array.ndim)


def params(**kw):
    return pltpu.CompilerParams(vmem_limit_bytes=VMEM_LIMIT, **kw)


def local(inputs, cotangent, region_id, spectral_w, conv_w, bias_vector):
    micro_count, _, rows_dev, channels, width = inputs.shape
    lanes = spectral_w.shape[-1]
    half = lanes // 2
    kx_dev = spectral_w.shape[1]
    row_devices, sections = lax.axis_size("rows"), lax.axis_size("section")
    mode_rows, height = kx_dev * row_devices, rows_dev * row_devices
    section = lax.axis_index("section")
    per_core = micro_count // sections
    kx_half = kx_dev // sections

    plain, doubled = col_tables(width, half)

    def stacked(array):
        high, low = np_split(array)
        return np.concatenate([high, high, low], 0)

    t_plain, t_doubled, it_plain, it_doubled = [stacked(t) for t in (plain, doubled, plain.T, doubled.T)]
    kron, ikron = row_tables(height, mode_rows, lax.axis_index("rows") * rows_dev, rows_dev)

    count = 2 * G
    chunks = channels // count
    hbm, vmem = pl.BlockSpec(memory_space=pl.ANY), pl.BlockSpec(memory_space=pltpu.VMEM)
    field_shape = jax.ShapeDtypeStruct((rows_dev, channels, width), F32)
    part_dims = (row_devices, chunks, sections, kx_half, count, lanes)
    p_shape, f_shape = jax.ShapeDtypeStruct(part_dims, F32), jax.ShapeDtypeStruct(part_dims[1:], F32)
    y_shape = jax.ShapeDtypeStruct((sections, chunks, kx_half, count, lanes), F32)
    stat_shape = jax.ShapeDtypeStruct((3, R, 128), F32)
    cg_shape = jax.ShapeDtypeStruct((2 * channels, 2 * channels), F32)
    bg_shape = jax.ShapeDtypeStruct((channels, width), F32)
    bound_shape = jax.ShapeDtypeStruct((micro_count, rows_dev, channels, width), F32)
    dma = pltpu.SemaphoreType.DMA
    field_buf = pltpu.VMEM((rows_dev, channels, width), F32)
    full_dims = (chunks, row_devices, sections, kx_half, count, lanes)
    spread = pltpu.VMEM((width // 128, rows_dev * count, 128), F32)
    energy = pltpu.VMEM((rows_dev, G, width), F32)
    line_sems = dma((2, chunks, row_devices))
    def run(body, ident, ins, outs, scratch, cost=50, aliases=None):
        names = [*ins, *outs, *scratch]
        spec = lambda entry: vmem if isinstance(entry, tuple) else hbm
        plain = lambda entry: entry[0] if isinstance(entry, tuple) else entry
        kernel = lambda *refs: body(types.SimpleNamespace(**dict(zip(names, refs))))
        positions = {list(ins).index(k): list(outs).index(v) for k, v in (aliases or {}).items()}
        result = pl.pallas_call(
            kernel, in_specs=[spec(e) for e in ins.values()], out_specs=[spec(e) for e in outs.values()],
            out_shape=[plain(e) for e in outs.values()], scratch_shapes=list(scratch.values()),
            input_output_aliases=positions,
            cost_estimate=pl.CostEstimate(flops=0, bytes_accessed=cost * 3_000_000, transcendentals=0),
            compiler_params=params(collective_id=ident, has_side_effects=True))(*[plain(e) for e in ins.values()])
        return types.SimpleNamespace(**dict(zip(outs, result)))

    conv_rows_at_once = 256 // channels
    maps = jnp.stack([conv_w[0].T, conv_w[0]])
    at = np.arange(conv_rows_at_once * channels) // channels
    wide_own = jnp.where(at[:, None] == at[None, :], jnp.tile(maps, (1, conv_rows_at_once, conv_rows_at_once)), 0.0)
    wide_own = jnp.stack(jnp.split(wide_own, wide_own.shape[2] // 128, 2), 1)
    bias_own = jnp.broadcast_to(bias_vector[0][:, None], (channels, width))

    streams = range(per_core)
    members = lax.axis_size("batch")
    kinds = ["middle", "turn", "back", "tail"]
    mixes = [(0, False), (1, False), (1, True), (0, True)]
    names = ["f00", "f01", "f10", "f11", "g10", "g11", "g00", "g01"]
    places = [dict(a=0, z=1), dict(a=2, z=3), dict(a=4, z=5, cot=6), dict(a=0, z=1, cot=2),
              dict(gz=3, a=4, h=5, dg=6), dict(gz=0, a=1, h=2, dg=3), dict(gz=4, a=5, h=6), dict(gz=0, a=1, h=2)]
    both = (2,)
    ins = dict(inputs=inputs, cotangent=cotangent, region=region_id, weights=spectral_w, t_plain=(t_plain,),
               t_doubled=(t_doubled,), it_plain=(it_plain,), it_doubled=(it_doubled,), kron=(kron,), ikron=(ikron,),
               wide_own=(wide_own,), bias_own=(bias_own,))
    outs = dict(far=jax.ShapeDtypeStruct((kx_half,) + spectral_w.shape[2:], F32), bound=bound_shape, stat=(jax.ShapeDtypeStruct((2 * per_core,) + stat_shape.shape, F32),),
                cg=(jax.ShapeDtypeStruct((2 * per_core,) + cg_shape.shape, F32),),
                bg=(jax.ShapeDtypeStruct((2 * per_core,) + bg_shape.shape, F32),),
                **{f"{name}{j}": field_shape for name in ("a1_", "dg0_", "gz1_", "ga1_", "gz0_") for j in streams},
                **{f"shared{i}": jax.ShapeDtypeStruct((members,) + f_shape.shape, F32) for i in range(len(names))})
    scratch = dict(
        fields=pltpu.VMEM((7,) + field_shape.shape, F32), full=pltpu.VMEM(both + full_dims, F32),
        part=pltpu.VMEM(both + part_dims, F32),
        come=pltpu.VMEM(both + (2, chunks, row_devices - 1) + part_dims[2:], F32),
        keep=pltpu.VMEM(both + f_shape.shape, F32), y_give=pltpu.VMEM(both + y_shape.shape[1:], F32),
        p_buf=pltpu.VMEM(full_dims, F32), spread=spread, eo=energy, eb=energy,
        rid=pltpu.VMEM((2, rows_dev, width), jnp.int32),
        wbuf=pltpu.VMEM((3, 2, count, channels, lanes), F32), macc=pltpu.VMEM((kx_half, 2 * sections, channels, lanes), F32),
        msrc=pltpu.VMEM((2 * sections, channels, lanes), F32),
        bias=pltpu.VMEM((2, channels, width), F32),
        conv=pltpu.VMEM((4, len(at), 3 * len(at)), BF16), m_cross=dma((2, 2)),
        field_sem=dma((7,)), rid_sem=dma(both), out_sem=dma((2, 2, chunks)), wsem=dma((3,)), w_load=dma((chunks, kx_half)), w_cross=dma((2, chunks, kx_half)),
        send=dma(both + (2, chunks, row_devices)), recv=dma(both + (2, chunks, row_devices)),
        red_send=dma(both + (2, chunks, row_devices)), red_recv=dma(both + (2, chunks, row_devices)),
        y_cross=dma((2, 2, chunks)), p_cross=dma((2, 2, chunks)),
        b_local=dma((2, chunks)), b_cross=dma((2, 2, chunks)),
        s_local=dma(both), s_send=dma((2, members)), s_recv=dma((len(names), members)))
    done = run(functools.partial(stages_kernel, per_core, kinds, places, mixes), 0, ins, outs, scratch, cost=400)
    gathered = {name: getattr(done, f"shared{i}") for i, name in enumerate(names)}
    bound, calls = done.bound, 0

    grids = per_core * members * sections
    block = 2 * G
    pairs, blocks = kx_half // 2, channels // block
    in_buf = pltpu.VMEM((2, per_core, members, chunks, sections, 2, count, lanes), F32)
    grad_scratch = dict(fbuf=in_buf, gbuf=in_buf, in_sem=dma((2, 2)), left_of=pltpu.VMEM((2, grids, lanes, lanes), F32),
                        right_of=pltpu.VMEM((grids, lanes, lanes), F32), product=pltpu.VMEM((half, lanes, lanes), F32))
    far_grad = run(functools.partial(far_grad_kernel, per_core), 1 + calls, gathered,
                   dict(far=jax.ShapeDtypeStruct((kx_half, channels, channels, lanes), F32)),
                   dict(out=pltpu.VMEM((2, 2, block, channels, lanes), F32), send=dma((pairs * blocks,)),
                        recv=dma((pairs * blocks,)), **grad_scratch)).far
    bound_rows = bound.reshape(micro_count * rows_dev, channels, width)
    bound_block = pl.BlockSpec((bound_rows.shape[0] // (pairs * blocks), channels, width),
                               lambda p, i, m: (p * blocks + i, 0, 0))
    grid_spec = pltpu.PrefetchScalarGridSpec(
        num_scalar_prefetch=1, grid=(pairs, blocks),
        in_specs=[hbm] * len(gathered)
        + [pl.BlockSpec((2, block, channels, lanes), lambda p, i, m: (p, i, 0, 0)), bound_block],
        out_specs=[pl.BlockSpec((2, 2, block, channels, lanes), lambda p, i, m: (0, p, i, 0, 0)), bound_block],
        scratch_shapes=list(grad_scratch.values()))
    spectral_grad, boundary = pl.pallas_call(
        functools.partial(own_grad_kernel, [*gathered, "far", "bound_in", "out", "bound_out", *grad_scratch], per_core),
        grid_spec=grid_spec, out_shape=[jax.ShapeDtypeStruct((2, kx_half, channels, channels, lanes), F32),
                                        jax.ShapeDtypeStruct(bound_rows.shape, F32)],
        cost_estimate=pl.CostEstimate(flops=0, bytes_accessed=150_000_000, transcendentals=0),
        compiler_params=params())(
            jnp.reshape(section, (1,)).astype(jnp.int32), *gathered.values(), far_grad, bound_rows)
    spectral_grad = spectral_grad.reshape(spectral_w.shape)
    boundary = boundary.reshape((1, micro_count, 1) + inputs.shape[2:])

    def lower(value):
        return (value[:channels, :channels] + value[channels:, channels:]
                + value[:channels, channels:] + value[channels:, :channels])

    pair = lambda value: jnp.sum(value.reshape((2, per_core) + value.shape[1:]), 1)
    conv_local = jnp.stack([lower(value) for value in pair(done.cg)[::-1]])
    bias_local = jnp.sum(pair(done.bg)[::-1], -1)
    stat_local = jnp.sum(pair(done.stat), -1)
    shapes = [v.shape for v in (conv_local, bias_local, stat_local)]
    flat_sums = jnp.concatenate([v.reshape(-1) for v in (conv_local, bias_local, stat_local)])
    length = flat_sums.shape[0]
    flat_sums = jnp.pad(flat_sums, (0, -length % 1024)).reshape(-1, 128)
    flat_sums = jnp.sum(lax.all_gather(flat_sums, ("section", "batch", "rows"), axis=0), 0).reshape(-1)
    ends = np.cumsum([0] + [math.prod(shape) for shape in shapes])
    conv_sum, bias_sum, stat_sum = [flat_sums[ends[i]:ends[i + 1]].reshape(shapes[i]) for i in range(3)]
    own_stat = lax.dynamic_index_in_dim(stat_sum, section, 0, False)
    layer_rms = jnp.sqrt(own_stat[:2] / (channels * own_stat[2])[None, :] + 1e-06)[None]
    own = lambda value: lax.dynamic_slice_in_dim(value, section, 1, 0)
    return boundary, spectral_grad, own(conv_sum), own(bias_sum), layer_rms


def solution(mesh):
    placed = (
        P(None, "batch", "rows", None, None),
        P(None, "batch", "rows", None, None),
        P(None, "batch", "rows", None),
        P("section", "rows", None, None, None),
        P("section", None, None),
        P("section", None),
    )
    return jax.shard_map(
        local,
        mesh=mesh,
        in_specs=placed,
        out_specs=(
            P("section", None, "batch", "rows", None, None),
            P("section", "rows", None, None, None),
            P("section", None, None),
            P("section", None),
            P("section", None, None),
        ),
        check_vma=False,
    )
```

profile of v0, /device:TPU:0, one launch (start us, length us, event | category | flops | bytes accessed | tf_op | source)
XLA Modules:
  0.0 666.1 jit_solution(10124136263869283527)
XLA Ops:
  7.2 0.0 copy-start
  7.2 0.0 all-gather.2.cloned.1.call-start
  7.2 0.8 copy.31
  8.1 0.8 pad_maximum_fusion.2
  8.8 0.1 copy.32
  8.9 0.2 fusion.10
  9.2 0.1 fusion.2
  9.3 0.7 copy.34.refs_8_
  10.0 0.9 copy.39
  10.9 0.1 tile.4
  11.0 0.6 tile.10
  11.6 0.1 broadcast_select_fusion
  11.7 0.7 pad_maximum_fusion.1.refs_9_
  12.5 0.8 pad_maximum_fusion.refs_10_
  13.3 0.0 copy-done
  13.3 0.7 broadcast_in_dim.23.refs_11_
  14.0 524.4 %shard_map.146 = (f32[8,64,64,128]{3,2,1,0:T(8,128)}, f32[4,64,64,256]{3,2,1,0:T(8,128)}, f32[4,3,8,128]{3,2,1,0:T(8,128)}, f32[4,128,128]{2,1,0:T(8,128)}, f32[...) custom-call(f32[4,1,64,64,256]{4,3,2,1,0:T(8,128)} %refs_0_.1, ...), custom_call_target="tpu_custom_call" | custom-call | bytes 1200000000 | tf_op jit(solution)/shard_map/pallas_call | solution.py:1110
  538.4 0.9 reduce_sum.59
  539.3 0.1 reshape.96
  539.4 1.0 bitcast_reduce_fusion.1
  540.4 0.1 fusion.8
  540.5 0.1 fusion.7
  540.6 0.1 reshape.93
  540.6 1.0 bitcast_reduce_fusion
  541.6 0.1 reverse_reduce_fusion
  541.7 0.1 reshape.95
  541.8 0.6 fusion.3
  542.4 0.0 all-gather.2.cloned.1.call-update
  542.5 51.7 %shard_map.147.refs_8_ = f32[8,64,64,128]{3,2,1,0:T(8,128)} custom-call(f32[4,4,2,8,16,128]{5,4,3,2,1,0:T(8,128)} %get-tuple-element.19.refs_0_, f32[4,4,2,8,16,128]{5,4,3,2,1,0:T(8,128)} %get-tuple-element.20.refs_1_, f32[4,4,2,8,16,128]{5,4,3,2,1,0:T(8,128)} %get-tuple-element.21.refs_2_, f32[4,4,2,8,16,128]{5,4,3,2,1,0:T(8,128)} %get-tuple-element.22.refs_3_, ...), custom_call_target="tpu_custom_call" | custom-call | bytes 150000000 | tf_op jit(solution)/shard_map/pallas_call | solution.py:1110
  594.2 61.2 %shard_map.148 = (f32[2,8,64,64,128]{4,3,2,1,0:T(8,128)}, f32[256,64,256]{2,1,0:T(8,128)}) custom-call(s32[1]{0:T(128)} %bitcast.m_ref, f32[4,4,2,8,16,128]{5,4,3,2,1,0:T(8,128)} %get-tuple-element.19.refs_0_, f32[4,4,2,8,16,128]{5,4,3,2,1,0:T(8,128)} %get-tuple-element.20.refs_1_, f32[4,4,2,8,16,128]{5,4,3,2,1,0:T(8,128)} %get-tuple-element.21.refs_2_, ...), custom_call_target="tpu_custom_call" | custom-call | bytes 150000000 | tf_op jit(solution)/shard_map/pallas_call | solution.py:1181
  655.4 0.0 all-gather.2.cloned.1.call-done
  655.4 1.3 reduce_sum.62
  656.8 0.1 reshape.98
  656.9 0.1 reshape.100
  657.0 0.5 constant_dynamic-slice_fusion.1
  657.5 0.6 add_sqrt_fusion
  658.1 0.1 reshape.97
  658.2 0.6 constant_dynamic-slice_fusion.2
  (11 shorter events, 0.1 us)
Async XLA Ops:
  7.2 6.1 copy-start
  7.2 648.2 %all-gather.2.cloned.1.call-start = ((), (), s32[]{:S(2)}) async-start(), calls=%async_computation | async-start | bytes 1216512 | tf_op jit(solution)/shard_map/all_gather | solution.py:1203
Sparse Core Ops, SparseCore 0:
  542.6 53.4 all-gather.1
where the time goes:
time: 676 us; the launch traced here: 666 us
  Pallas kernels  637 us (94%)
  between operations  14.6 us (2%)
  other arithmetic  8.38 us (1%)
    pallas_call x2, Pallas kernels, run(): pl.pallas_call(kernel, in_specs=[spec(e) for e in ins.values()], out_spec...  576 us
    pallas_call x1, Pallas kernels, local(): pl.pallas_call(functools.partial(own_grad_kernel, [*gathered, 'far', 'bou...  61.2 us
  transfers between devices with their start and end apart: 1, of which 0 were waited for; matrix products, arithmetic and copies ran while one was open for 0% of the time, Pallas kernels for 17%

commit v1 on v0

--- a/solution.py
+++ b/solution.py
@@ -12,7 +12,6 @@
 
 R = 8
 G = 8
-AHEAD = 2
 F32 = jnp.float32
 BF16 = jnp.bfloat16
 VMEM_LIMIT = 62 * 1024 * 1024
@@ -222,15 +221,8 @@
                 def _():
                     self.hop(way, q, hop + 1).start()
 
-    def begin(self):
-        for q in range(min(AHEAD, self.chunks)):
-            self.own(q)
-
     def tick(self, t):
-        @pl.when(t + AHEAD < self.chunks)
-        def _():
-            self.own(t + AHEAD)
-
+        pl.when(within(t, self.chunks))(functools.partial(self.own, t))
         for hop in range(self.n - 1):
             q = t - hop - 1
             pl.when(within(q, self.chunks))(functools.partial(self.step, q, hop))
@@ -268,21 +260,19 @@
 
     def first(self, q):
         self.admit(q)
-        for way in range(2):
-            @pl.when(jnp.logical_not(self.hears(way)))
-            def _():
-                for hop in range(1, self.n):
-                    @pl.when(self.valid(way, hop))
-                    def _():
-                        self.sent(way, q, hop).start()
+        self.step(q, 1)
 
     def step(self, q, hop):
         for way in range(2):
-            @pl.when(jnp.logical_and(self.valid(way, hop), self.hears(way)))
+            @pl.when(self.valid(way, hop))
             def _():
-                self.heard(way, q, hop - 1)
-                owner = self.owner(way, hop)
-                self.part[owner, q] = self.part[owner, q] + self.come[way, q, hop - 2]
+                if hop > 1:
+                    @pl.when(self.hears(way))
+                    def _():
+                        self.heard(way, q, hop - 1)
+                        owner = self.owner(way, hop)
+                        self.part[owner, q] = self.part[owner, q] + self.come[way, q, hop - 2]
+
                 self.sent(way, q, hop).start()
 
     def final(self, q):
@@ -720,7 +710,6 @@
             mix.prime()
         lead = n - 1 if k == 0 else chunks - 1
         ready = n - 1 - lead
-        gather.begin()
         stage.open()
 
         def early(i, carry):

time: 676 us -> 660 us (0.976)
  Pallas kernels: 637 us -> 622 us
    pallas_call x2, Pallas kernels: 576 us -> 560 us  [run(): pl.pallas_call(kernel, in_specs=[spec(e) for e in ins.values()], out_spec...]
where the time goes in v1:
time: 660 us; the launch traced here: 650 us
  Pallas kernels  622 us (94%)
  between operations  14.6 us (2%)
  other arithmetic  8.39 us (1%)
    pallas_call x2, Pallas kernels, run(): pl.pallas_call(kernel, in_specs=[spec(e) for e in ins.values()], out_spec...  560 us
    pallas_call x1, Pallas kernels, local(): pl.pallas_call(functools.partial(own_grad_kernel, [*gathered, 'far', 'bou...  61.2 us
  transfers between devices with their start and end apart: 1, of which 0 were waited for; matrix products, arithmetic and copies ran while one was open for 0% of the time, Pallas kernels for 17%

profile of v1, /device:TPU:0, one launch (start us, length us, event | category | flops | bytes accessed | tf_op | source)
XLA Modules:
  0.0 650.4 jit_solution(11837099915117677043)
XLA Ops:
  7.2 0.0 copy-start
  7.2 0.0 all-gather.2.cloned.1.call-start
  7.2 0.8 copy.31
  8.1 0.8 pad_maximum_fusion.2
  8.8 0.1 copy.32
  8.9 0.2 fusion.10
  9.2 0.1 fusion.2
  9.3 0.7 copy.34.refs_8_
  10.0 0.9 copy.39
  10.9 0.1 tile.4
  11.0 0.6 tile.10
  11.6 0.1 broadcast_select_fusion
  11.7 0.7 pad_maximum_fusion.1.refs_9_
  12.5 0.8 pad_maximum_fusion.refs_10_
  13.3 0.0 copy-done
  13.3 0.7 broadcast_in_dim.23.refs_11_
  14.0 508.9 %shard_map.146 = (f32[8,64,64,128]{3,2,1,0:T(8,128)}, f32[4,64,64,256]{3,2,1,0:T(8,128)}, f32[4,3,8,128]{3,2,1,0:T(8,128)}, f32[4,128,128]{2,1,0:T(8,128)}, f32[...) custom-call(f32[4,1,64,64,256]{4,3,2,1,0:T(8,128)} %refs_0_.1, ...), custom_call_target="tpu_custom_call" | custom-call | bytes 1200000000 | tf_op jit(solution)/shard_map/pallas_call | solution.py:1099
  522.9 0.9 reduce_sum.59
  523.8 0.1 reshape.96
  523.9 1.0 bitcast_reduce_fusion.1
  524.9 0.1 fusion.8
  525.0 0.1 fusion.7
  525.1 0.1 reshape.93
  525.1 1.0 bitcast_reduce_fusion
  526.1 0.1 reverse_reduce_fusion
  526.2 0.1 reshape.95
  526.3 0.6 fusion.3
  526.9 0.0 all-gather.2.cloned.1.call-update
  527.0 51.6 %shard_map.147.refs_8_ = f32[8,64,64,128]{3,2,1,0:T(8,128)} custom-call(f32[4,4,2,8,16,128]{5,4,3,2,1,0:T(8,128)} %get-tuple-element.19.refs_0_, f32[4,4,2,8,16,128]{5,4,3,2,1,0:T(8,128)} %get-tuple-element.20.refs_1_, f32[4,4,2,8,16,128]{5,4,3,2,1,0:T(8,128)} %get-tuple-element.21.refs_2_, f32[4,4,2,8,16,128]{5,4,3,2,1,0:T(8,128)} %get-tuple-element.22.refs_3_, ...), custom_call_target="tpu_custom_call" | custom-call | bytes 150000000 | tf_op jit(solution)/shard_map/pallas_call | solution.py:1099
  578.6 61.2 %shard_map.148 = (f32[2,8,64,64,128]{4,3,2,1,0:T(8,128)}, f32[256,64,256]{2,1,0:T(8,128)}) custom-call(s32[1]{0:T(128)} %bitcast.m_ref, f32[4,4,2,8,16,128]{5,4,3,2,1,0:T(8,128)} %get-tuple-element.19.refs_0_, f32[4,4,2,8,16,128]{5,4,3,2,1,0:T(8,128)} %get-tuple-element.20.refs_1_, f32[4,4,2,8,16,128]{5,4,3,2,1,0:T(8,128)} %get-tuple-element.21.refs_2_, ...), custom_call_target="tpu_custom_call" | custom-call | bytes 150000000 | tf_op jit(solution)/shard_map/pallas_call | solution.py:1170
  639.8 0.0 all-gather.2.cloned.1.call-done
  639.8 1.3 reduce_sum.62
  641.2 0.1 reshape.98
  641.3 0.1 reshape.100
  641.3 0.5 constant_dynamic-slice_fusion.1
  641.9 0.6 add_sqrt_fusion
  642.5 0.1 reshape.97
  642.5 0.6 constant_dynamic-slice_fusion.2
  (11 shorter events, 0.1 us)
Async XLA Ops:
  7.2 6.1 copy-start
  7.2 632.6 %all-gather.2.cloned.1.call-start = ((), (), s32[]{:S(2)}) async-start(), calls=%async_computation | async-start | bytes 1216512 | tf_op jit(solution)/shard_map/all_gather | solution.py:1192
Sparse Core Ops, SparseCore 0:
  527.1 56.0 all-gather.1

commit v2 on v1

--- a/solution.py
+++ b/solution.py
@@ -221,8 +221,10 @@
                 def _():
                     self.hop(way, q, hop + 1).start()
 
-    def tick(self, t):
+    def free(self, t):
         pl.when(within(t, self.chunks))(functools.partial(self.own, t))
+
+    def rest(self, t):
         for hop in range(self.n - 1):
             q = t - hop - 1
             pl.when(within(q, self.chunks))(functools.partial(self.step, q, hop))
@@ -260,19 +262,21 @@
 
     def first(self, q):
         self.admit(q)
-        self.step(q, 1)
+        self.launch(q, 1)
+
+    def launch(self, q, hop):
+        for way in range(2):
+            @pl.when(jnp.logical_and(self.valid(way, hop), jnp.logical_not(self.hears(way))))
+            def _():
+                self.sent(way, q, hop).start()
 
     def step(self, q, hop):
         for way in range(2):
-            @pl.when(self.valid(way, hop))
+            @pl.when(jnp.logical_and(self.valid(way, hop), self.hears(way)))
             def _():
-                if hop > 1:
-                    @pl.when(self.hears(way))
-                    def _():
-                        self.heard(way, q, hop - 1)
-                        owner = self.owner(way, hop)
-                        self.part[owner, q] = self.part[owner, q] + self.come[way, q, hop - 2]
-
+                self.heard(way, q, hop - 1)
+                owner = self.owner(way, hop)
+                self.part[owner, q] = self.part[owner, q] + self.come[way, q, hop - 2]
                 self.sent(way, q, hop).start()
 
     def final(self, q):
@@ -284,12 +288,21 @@
 
         self.keep[q] = self.part[self.z, q]
 
-    def tick(self, t):
+    def free(self, t):
         pl.when(within(t, self.chunks))(functools.partial(self.first, t))
+        for hop in range(2, self.n):
+            q = t - hop + 1
+            pl.when(within(q, self.chunks))(functools.partial(self.launch, q, hop))
+
+    def rest(self, t):
         for hop in range(2, self.n + 1):
             q = t - hop + 1
             pl.when(within(q, self.chunks))(
                 functools.partial(self.step, q, hop) if hop < self.n else functools.partial(self.final, q))
+
+    def tick(self, t):
+        self.free(t)
+        self.rest(t)
 
     def finish(self):
         def body(q, carry):
@@ -713,9 +726,10 @@
         stage.open()
 
         def early(i, carry):
+            gather.free(i)
             if sums is not None:
                 sums.tick(i + lead)
-            gather.tick(i)
+            gather.rest(i)
             stage.before(i)
             if mix is not None and not mix.flip:
                 pl.when(within(i - ready, chunks))(lambda: mix.chunk(i - ready))
@@ -730,11 +744,14 @@
 
         def later(q, carry):
             i = q + n - 1
+            gather.free(i)
+            if now is not None:
+                now.free(i - n)
             if sums is not None:
                 sums.tick(i + lead)
             if now is not None:
-                now.tick(i - n)
-            gather.tick(i)
+                now.rest(i - n)
+            gather.rest(i)
             stage.chunk(q)
             if mix is not None:
                 if mix.flip:
@@ -825,9 +842,21 @@
 
             return carry
 
+        if self.flip:
+            pl.when(q == 0)(self.sources)
         lax.fori_loop(0, self.half, body, 0)
         if self.flip:
             self.gather.give(q)
+
+    def sources(self):
+        def body(x, carry):
+            for g in range(self.grids):
+                value = jnp.concatenate([self.sums.part[self.z, at, g, x] for at in range(self.chunks)], 0)
+                self.r.macc[x, 2 * g] = value
+                self.r.macc[x, 2 * g + 1] = swap_halves(value)
+            return carry
+
+        lax.fori_loop(0, self.half, body, 0)
 
     def forward(self, q, x, weight):
         sides, groups = 2 * self.grids, self.channels // G
@@ -855,12 +884,7 @@
 
     def transposed(self, q, x, weight):
         sides, groups = 2 * self.grids, self.channels // G
-        source = self.r.msrc
-        for g in range(self.grids):
-            value = jnp.concatenate([self.sums.part[self.z, at, g, x] for at in range(self.chunks)], 0)
-            source[2 * g] = value
-            source[2 * g + 1] = swap_halves(value)
-        rows = [pieces(source[k]) for k in range(sides)]
+        rows = [pieces(self.r.macc[x, k]) for k in range(sides)]
         out = [[] for _ in range(sides)]
         for i in range(self.count):
             total = [None] * sides

time: 660 us -> 664 us (level)
  no operation moved by 1% of the time
where the time goes in v2:
time: 664 us; the launch traced here: 655 us
  Pallas kernels  626 us (94%)
  between operations  14.6 us (2%)
  other arithmetic  8.38 us (1%)
    pallas_call x2, Pallas kernels, run(): pl.pallas_call(kernel, in_specs=[spec(e) for e in ins.values()], out_spec...  565 us
    pallas_call x1, Pallas kernels, local(): pl.pallas_call(functools.partial(own_grad_kernel, [*gathered, 'far', 'bou...  61.2 us
  transfers between devices with their start and end apart: 1, of which 0 were waited for; matrix products, arithmetic and copies ran while one was open for 0% of the time, Pallas kernels for 17%

profile of v2, /device:TPU:0, one launch (start us, length us, event | category | flops | bytes accessed | tf_op | source)
XLA Modules:
  0.0 654.8 jit_solution(7881998186843663753)
XLA Ops:
  7.2 0.0 copy-start
  7.2 0.0 all-gather.2.cloned.1.call-start
  7.2 0.8 copy.31
  8.1 0.8 pad_maximum_fusion.2
  8.8 0.1 copy.32
  8.9 0.2 fusion.10
  9.2 0.1 fusion.2
  9.3 0.7 copy.34.refs_8_
  10.0 0.9 copy.39
  10.9 0.1 tile.4
  11.0 0.6 tile.10
  11.6 0.1 broadcast_select_fusion
  11.7 0.7 pad_maximum_fusion.1.refs_9_
  12.5 0.8 pad_maximum_fusion.refs_10_
  13.3 0.0 copy-done
  13.3 0.7 broadcast_in_dim.23.refs_11_
  14.0 513.2 %shard_map.146 = (f32[8,64,64,128]{3,2,1,0:T(8,128)}, f32[4,64,64,256]{3,2,1,0:T(8,128)}, f32[4,3,8,128]{3,2,1,0:T(8,128)}, f32[4,128,128]{2,1,0:T(8,128)}, f32[...) custom-call(f32[4,1,64,64,256]{4,3,2,1,0:T(8,128)} %refs_0_.1, ...), custom_call_target="tpu_custom_call" | custom-call | bytes 1200000000 | tf_op jit(solution)/shard_map/pallas_call | solution.py:1123
  527.1 0.9 reduce_sum.59
  528.1 0.1 reshape.96
  528.1 1.0 bitcast_reduce_fusion.1
  529.1 0.1 fusion.8
  529.2 0.1 fusion.7
  529.3 0.1 reshape.93
  529.4 1.0 bitcast_reduce_fusion
  530.4 0.1 reverse_reduce_fusion
  530.5 0.1 reshape.95
  530.6 0.6 fusion.3
  531.2 0.0 all-gather.2.cloned.1.call-update
  531.2 51.7 %shard_map.147.refs_8_ = f32[8,64,64,128]{3,2,1,0:T(8,128)} custom-call(f32[4,4,2,8,16,128]{5,4,3,2,1,0:T(8,128)} %get-tuple-element.19.refs_0_, f32[4,4,2,8,16,128]{5,4,3,2,1,0:T(8,128)} %get-tuple-element.20.refs_1_, f32[4,4,2,8,16,128]{5,4,3,2,1,0:T(8,128)} %get-tuple-element.21.refs_2_, f32[4,4,2,8,16,128]{5,4,3,2,1,0:T(8,128)} %get-tuple-element.22.refs_3_, ...), custom_call_target="tpu_custom_call" | custom-call | bytes 150000000 | tf_op jit(solution)/shard_map/pallas_call | solution.py:1123
  582.9 61.2 %shard_map.148 = (f32[2,8,64,64,128]{4,3,2,1,0:T(8,128)}, f32[256,64,256]{2,1,0:T(8,128)}) custom-call(s32[1]{0:T(128)} %bitcast.m_ref, f32[4,4,2,8,16,128]{5,4,3,2,1,0:T(8,128)} %get-tuple-element.19.refs_0_, f32[4,4,2,8,16,128]{5,4,3,2,1,0:T(8,128)} %get-tuple-element.20.refs_1_, f32[4,4,2,8,16,128]{5,4,3,2,1,0:T(8,128)} %get-tuple-element.21.refs_2_, ...), custom_call_target="tpu_custom_call" | custom-call | bytes 150000000 | tf_op jit(solution)/shard_map/pallas_call | solution.py:1194
  644.1 0.0 all-gather.2.cloned.1.call-done
  644.2 1.3 reduce_sum.62
  645.6 0.1 reshape.98
  645.6 0.1 reshape.100
  645.7 0.5 constant_dynamic-slice_fusion.1
  646.3 0.6 add_sqrt_fusion
  646.8 0.1 reshape.97
  646.9 0.6 constant_dynamic-slice_fusion.2
  (11 shorter events, 0.1 us)
Async XLA Ops:
  7.2 6.1 copy-start
  7.2 637.0 %all-gather.2.cloned.1.call-start = ((), (), s32[]{:S(2)}) async-start(), calls=%async_computation | async-start | bytes 1216512 | tf_op jit(solution)/shard_map/all_gather | solution.py:1216
Sparse Core Ops, SparseCore 0:
  531.3 54.0 all-gather.1
